TPU v7x, 256 devices: a whole 4x4x8 slice. The times are simulated.
256 devices in a mesh: pa: 16 (over x, z_lo, core), pb: 16 (over y, z_hi).
Axes of the slice: x: 4, y: 4, z: 8 (z_hi: 4, z_lo: 2; z = z_hi * 2 + z_lo), core: 2. Of those that a mesh axis runs over, the one named last changes fastest.
Arguments:
- point_keys: bfloat16 [32768, 768], P(('pa', 'pb')), may hold values from -7 to 7
- point_values: bfloat16 [32768, 768], P(('pa', 'pb')), may hold values from -40 to 40
- out_grad: bfloat16 [32768, 768], P(('pa', 'pb')), may hold values from -512 to 512
- decoder_norm: float32 [12, 32768], P(None, ('pa', 'pb')), as said below
- latent_query: bfloat16 [1024, 768], P(('pa', 'pb')), may hold values from -4 to 4
- latent_out: bfloat16 [1024, 768], P(('pa', 'pb')), may hold values from -5 to 5
- encoder_norm: float32 [12, 1024], replicated, as said below
Outputs:
- keys_grad: bfloat16 [32768, 768], P(('pa', 'pb'))
- values_grad: bfloat16 [32768, 768], P(('pa', 'pb'))
- latent_grad: float32 [1024, 768], P(('pa', 'pb'))
Inputs may be any that keep to these rules, and one draw needn't show every extreme that they name: `decoder_norm`: each entry lies between log(1024) - 0.3 and log(1024) + 1.3. `encoder_norm`: each entry lies between log(32768) - 0.3 and log(32768) + 1.3.
All inputs are finite; a program needn't handle non-finite values.
Results may differ from a plain program's by a relative error of at most 0.004.
The roundings to bfloat16 on the way count: a program that leaves them out, or rounds other values in their place, can miss the bound.
Values may be sent and summed in bfloat16 or wider, within the bound.
A program may use at most 64 MiB of HBM per device.

v0:
```python
import jax
import jax.numpy as jnp
from jax import lax
from jax.sharding import PartitionSpec as P

HEADS = 12
HEAD_DIM = 64


def in_one_piece(arrays, axis, dim, along):
    widths = [a.shape[along] for a in arrays]
    both = jnp.concatenate(arrays, axis=along)
    result = lax.all_gather(both, axis, axis=dim, tiled=True)
    return tuple(jnp.split(result, [sum(widths[:k]) for k in range(1, len(widths))], axis=along))


def column(block, current):
    return lax.dynamic_slice_in_dim(block, current * HEAD_DIM, HEAD_DIM, 1)


def put_head(total, piece, current):
    return lax.dynamic_update_slice_in_dim(total, piece, current * HEAD_DIM, 1)


def add_head(total, piece, current):
    return put_head(total, column(total, current) + piece, current)


def across(left, right):
    return lax.dot_general(
        left, right, (((1,), (1,)), ((), ())), preferred_element_type=jnp.float32
    )


def down_rows(left, right):
    return lax.dot_general(
        left, right, (((0,), (0,)), ((), ())), preferred_element_type=jnp.float32
    )


def shards(
    point_keys, point_values, out_grad, decoder_norm, latent_query, latent_out, encoder_norm
):
    scale_factor = HEAD_DIM ** (-0.5)
    lat_all, out_all = in_one_piece((latent_query, latent_out), ("pa", "pb"), 0, 1)
    point_rows = point_keys.shape[0]
    latent_rows = lat_all.shape[0]
    width = point_keys.shape[1]

    def encoder_row(current):
        return lax.dynamic_slice_in_dim(encoder_norm, current, 1, 0)

    def pass_one(current, state):
        mix_acc, query_acc, key_acc, weighted_acc = state
        key_head = column(point_keys, current)
        grad_head = column(out_grad, current)
        lat_head = column(lat_all, current)
        scores = across(key_head, lat_head) * scale_factor
        decoder_weights = jnp.exp(scores - lax.dynamic_slice_in_dim(decoder_norm, current, 1, 0).T)
        decoder_gradient = across(grad_head, column(out_all, current))
        row_total = jnp.sum(decoder_weights * decoder_gradient, axis=1, keepdims=True)
        decoder_scores_grad = (decoder_weights * (decoder_gradient - row_total)).astype(
            jnp.bfloat16
        )
        mix_acc = put_head(
            mix_acc, down_rows(decoder_weights.astype(jnp.bfloat16), grad_head), current
        )
        query_acc = put_head(
            query_acc, down_rows(decoder_scores_grad, key_head) * scale_factor, current
        )
        key_acc = put_head(
            key_acc,
            jnp.dot(decoder_scores_grad, lat_head, preferred_element_type=jnp.float32)
            * scale_factor,
            current,
        )
        return (mix_acc, query_acc, key_acc, weighted_acc)

    weighted_blank = jnp.zeros((1, 1), jnp.float32)
    latent_blank = jnp.zeros((latent_rows, width), jnp.float32)
    begin = (
        latent_blank,
        latent_blank,
        jnp.zeros((point_rows, width), jnp.float32),
        weighted_blank,
    )
    mix_acc, query_acc, key_acc, weighted_acc = lax.fori_loop(0, HEADS, pass_one, begin)
    mix_grad = lax.psum(mix_acc, ("pa", "pb"))
    mixing_portion = mix_grad.astype(jnp.bfloat16)

    def pass_two(current, state):
        partial_rows, value_acc = state
        scores = across(column(point_keys, current), column(lat_all, current)) * scale_factor
        encoder_portion = jnp.exp(scores - encoder_row(current)).astype(jnp.bfloat16)
        mix_head = column(mixing_portion, current)
        encoder_gradient = across(column(point_values, current), mix_head)
        sums = jnp.sum(encoder_portion.astype(jnp.float32) * encoder_gradient, axis=0)[None, :]
        partial_rows = lax.dynamic_update_slice_in_dim(partial_rows, sums, current, 0)
        value_acc = put_head(
            value_acc,
            jnp.dot(encoder_portion, mix_head, preferred_element_type=jnp.float32),
            current,
        )
        return (partial_rows, value_acc)

    partial_rows, value_acc = lax.fori_loop(
        0,
        HEADS,
        pass_two,
        (jnp.zeros((HEADS, latent_rows), jnp.float32), jnp.zeros((point_rows, width), jnp.float32)),
    )
    column_total = lax.psum(partial_rows, ("pa", "pb"))

    def pass_three(current, state):
        query_acc, key_acc, value_acc = state
        key_head = column(point_keys, current)
        lat_head = column(lat_all, current)
        mix_head = column(mixing_portion, current)
        scores = across(key_head, lat_head) * scale_factor
        encoder = jnp.exp(scores - encoder_row(current))
        encoder_gradient = across(column(point_values, current), mix_head)
        encoder_scores_grad = (
            encoder * (encoder_gradient - lax.dynamic_slice_in_dim(column_total, current, 1, 0))
        ).astype(jnp.bfloat16)
        query_acc = add_head(
            query_acc, down_rows(encoder_scores_grad, key_head) * scale_factor, current
        )
        key_acc = add_head(
            key_acc,
            jnp.dot(encoder_scores_grad, lat_head, preferred_element_type=jnp.float32)
            * scale_factor,
            current,
        )
        return (query_acc, key_acc, value_acc)

    query_acc, key_acc, value_acc = lax.fori_loop(
        0, HEADS, pass_three, (query_acc, key_acc, value_acc)
    )
    latent_grad = lax.psum_scatter(query_acc, ("pa", "pb"), scatter_dimension=0, tiled=True)
    return (key_acc.astype(jnp.bfloat16), value_acc.astype(jnp.bfloat16), latent_grad)


def solution(mesh):
    in_specs = (
        P(("pa", "pb"), None),
        P(("pa", "pb"), None),
        P(("pa", "pb"), None),
        P(None, ("pa", "pb")),
        P(("pa", "pb"), None),
        P(("pa", "pb"), None),
        P(),
    )
    out_specs = (P(("pa", "pb"), None), P(("pa", "pb"), None), P(("pa", "pb"), None))
    return jax.shard_map(shards, mesh=mesh, in_specs=in_specs, out_specs=out_specs, check_vma=False)
```

profile of v0, /device:TPU:8, one launch (start us, length us, event | category | flops | bytes accessed | tf_op | source)
XLA Modules:
  0.0 1422.6 jit_solution(10542835375838273922)
XLA Ops:
  9.3 681.7 %all-gather.3.cloned.1.call-done = bf16[256,4,1536]{2,1,0:T(4,128)(2,1)} async-done(((bf16[1,4,1536]{2,1,0:T(4,128)(2,1)}), bf16[256,4,1536]{2,1,0:T(4,128)(2,1)}) %all-gather.3.cloned.1.call-update) | async-done | bytes 3145744 | tf_op jit(solution)/shard_map/all_gather | solution.py:13
  691.0 5.9 reshape.9
  696.8 2.1 fusion.49
  698.9 2.1 broadcast_in_dim.16
  701.0 2.1 broadcast_in_dim.16.clone
  703.1 84.2 %while.47 = (s32[]{:T(128)}, f32[1024,768]{0,1:T(8,128)}, f32[1024,768]{0,1:T(8,128)}, f32[128,768]{0,1:T(8,128)S(1)}, bf16[128,768]{1,0:T(8,128)(2,1)}, /*index...) while((s32[]{:T(128)}, f32[1024,768]{0,1:T(8,128)}, ...), condition=%wide.region_2.0_spmd, body=%wide.region_0.0_spmd.sunk | while | flops 85008256 | bytes 5414575 | solution.py:87
  706.2 1.8 fusion.96
  713.2 1.8 fusion.96
  727.2 1.8 fusion.96
  755.3 1.8 fusion.96
  764.1 1.8 convolution_dynamic-update-slice_fusion.4
  769.3 1.8 fusion.96
  783.3 1.8 fusion.96
  787.3 3.6 copy.14
  790.9 155.3 %all-reduce.5 = bf16[1024,768]{1,0:T(8,128)(2,1)S(1)} all-reduce(f32[1024,768]{1,0:T(8,128)} %copy.14), channel_id=1, replica_groups=mesh['pa'=16,'pb'=16] {'pa','pb'}, use_global_device_ids=true, to_apply=%region_3.0 | all-reduce | flops 786432 | bytes 4718592 | tf_op jit(solution)/shard_map/psum | solution.py:88
  946.2 64.0 %while.48 = (s32[]{:T(128)}, f32[12,1024]{1,0:T(8,128)}, bf16[128,768]{0,1:T(8,128)(2,1)}, bf16[128,768]{1,0:T(8,128)(2,1)}, bf16[1024,768]{1,0:T(8,128)(2,1)S(1...) while((s32[]{:T(128)}, f32[12,1024]{1,0:T(8,128)}, ...), condition=%wide.region_6.0_spmd, body=%wide.region_4.0_spmd.sunk | while | flops 51117060 | bytes 1698987 | solution.py:106
  1010.2 73.7 %psum.15 = f32[12,1024]{1,0:T(8,128)} all-reduce(f32[12,1024]{1,0:T(8,128)} %get-tuple-element.457), channel_id=1, replica_groups=mesh['pa'=16,'pb'=16] {'pa','pb'}, use_global_device_ids=true, to_apply=%region_7.0 | all-reduce | flops 12288 | bytes 98304 | tf_op jit(solution)/shard_map/psum | solution.py:112
  1083.9 64.4 %while.49 = (s32[]{:T(128)}, f32[1024,768]{0,1:T(8,128)}, f32[128,768]{0,1:T(8,128)S(1)}, bf16[128,768]{1,0:T(8,128)(2,1)}, bf16[1024,768]{1,0:T(8,128)(2,1)S(1)...) while((s32[]{:T(128)}, f32[1024,768]{0,1:T(8,128)}, ...), condition=%wide.region_9.0_spmd, body=%wide.region_8.0_spmd.sunk | while | flops 67911680 | bytes 3338415 | solution.py:136
  1086.9 2.0 fusion.115
  1092.3 2.0 fusion.115
  1097.6 2.0 fusion.115
  1103.0 2.0 fusion.115
  1108.4 2.0 fusion.115
  1113.7 2.0 fusion.115
  1119.1 2.0 fusion.115
  1124.4 2.0 fusion.115
  1129.8 2.0 fusion.115
  1135.2 2.0 fusion.115
  1140.6 2.0 fusion.115
  1145.9 2.0 fusion.115
  1148.3 3.6 copy.17
  1153.6 260.8 %all-reduce.4.cloned.1.call-done = f32[1024,768]{1,0:T(8,128)} async-done(((f32[1024,768]{1,0:T(8,128)}), f32[1024,768]{1,0:T(8,128)}) %all-reduce.4.cloned.1.call-update) | async-done | bytes 3145744
  (198 shorter events, 180.2 us)
Async XLA Ops:
  7.2 683.8 %all-gather.3.cloned.1.call-start = ((), (), s32[]{:S(2)}) async-start(), calls=%async_computation | async-start | bytes 3158016 | tf_op jit(solution)/shard_map/all_gather | solution.py:13
  8.6 1405.9 %all-reduce.4.cloned.1.call-start = ((), (), s32[]{:S(2)}) async-start(), calls=%async_computation.1 | async-start | bytes 6291456
  1151.9 0.9 copy-start
Sparse Core Ops, SparseCore 0:
  10.4 680.4 all-gather.2
  1152.0 262.3 all-reduce.3
where the time goes:
time: 1430 us; the launch traced here: 1420 us
  waiting for transfers between devices  942 us (66%)
  blocking collectives  229 us (16%)
  matrix products  166 us (12%)
  local copies, waits for them, and re-layouts  66.2 us (5%)
    all_gather x1, waiting for transfers between devices, in_one_piece(): result = lax.all_gather(both, axis, axis=dim, tiled=True)  682 us
    unnamed x3, waiting for transfers between devices  261 us
    psum x1, blocking collectives, shards(): mix_grad = lax.psum(mix_acc, ('pa', 'pb'))  155 us
    dot_general x72, matrix products, across(): lax.dot_general(left, right, (((1,), (1,)), ((), ())), preferred_element_...  79.1 us
    psum x1, blocking collectives, shards(): column_total = lax.psum(partial_rows, ('pa', 'pb'))  73.7 us
    dot_general x36, matrix products, down_rows(): lax.dot_general(left, right, (((0,), (0,)), ((), ())), preferred_element_...  66.2 us
  transfers between devices with their start and end apart: 2, of which 2 were waited for; matrix products, arithmetic and copies ran while one was open for 0% of the time, Pallas kernels for 0%

commit v1 on v0

v1 whole, which is shorter than its diff:
```python
import jax
import jax.numpy as jnp
from jax import lax
from jax.experimental import pallas as pl
from jax.experimental.pallas import tpu as pltpu
from jax.sharding import PartitionSpec as P

HEADS = 12
HEAD_DIM = 64
SLOTS = 16
PTS = 128
BLOCK = 64
CHUNK = 4
CROWS = CHUNK * BLOCK
NB = 4
NW = 512
MESH = pl.DeviceIdType.MESH
F32 = jnp.float32
BF16 = jnp.bfloat16


def dot(a, b):
    return jnp.dot(a, b, preferred_element_type=F32)


def three_terms(v):
    one = v.astype(BF16).astype(F32)
    two = (v - one).astype(BF16).astype(F32)
    three = (v - one - two).astype(BF16).astype(F32)
    return one, two, three


def iota(shape, dim):
    return lax.broadcasted_iota(jnp.int32, shape, dim)


def kernel(
    keys_ref, values_ref, grad_ref, dnorm_ref, query_ref, lout_ref, enorm_ref,
    kout_ref, vout_ref, lgout_ref,
    send_lat, send_pts, tall, got_lat, got_pts,
    key_rows, grad_rows, value_rows, key_grad, value_cols, dnorm, enorm,
    lat, lat_turned, dec, enc, dgrad, query_acc,
    mixu, from_core, summed, from_z, mix_all, keys_t, values_t,
    lg_part, lg_core, lg_summed, lg_z, lg_own, kv_send, kv_got, lg_got,
    s_lat, r_lat, s_pts, r_pts, s_all, r_all, s_core, r_core, s_z, r_z,
    s_mix, r_mix, s_core2, r_core2, s_z2, r_z2, s_kv, r_kv, s_lg, r_lg,
):
    pa, pb = lax.axis_index("pa"), lax.axis_index("pb")
    x, zlo, c = pa // 4, (pa // 2) % 2, pa % 2
    y, zhi = pb // 4, pb % 4
    z = zhi * 2 + zlo
    slot = x * 4 + y
    member = c * 8 + z

    def in_plane(t):
        return ((t // 4) * 4 + zlo * 2 + c, (t % 4) * 4 + zhi)

    def in_column(g):
        cc, zz = g // 8, g % 8
        return (x * 4 + (zz % 2) * 2 + cc, y * 4 + zz // 2)

    def remote(src, dst, s, r, to):
        return pltpu.make_async_remote_copy(
            src_ref=src, dst_ref=dst, send_sem=s, recv_sem=r, device_id=to, device_id_type=MESH
        )

    def loop(lo, hi, body):
        def step(i, carry):
            body(i)
            return carry

        lax.fori_loop(lo, hi, step, 0)

    barrier = pltpu.get_barrier_semaphore()

    def greet(k):
        pl.semaphore_signal(barrier, inc=1, device_id=in_plane((slot + k) % SLOTS), device_id_type=MESH)
        pl.semaphore_signal(barrier, inc=1, device_id=in_column((member + k) % SLOTS), device_id_type=MESH)

    loop(1, SLOTS, greet)

    for k in range(4):
        tall[0, 4 * k : 4 * k + 4, :] = query_ref[...].astype(F32) * 0.125
        tall[1, 4 * k : 4 * k + 4, :] = lout_ref[...].astype(F32)
    rows16 = iota((16, 128), 0)
    left16 = iota((16, 128), 1) < HEAD_DIM
    mine = rows16 // 4 == y
    for p in range(HEADS // 2):
        q = tall[0, :, 128 * p : 128 * p + 128]
        o = tall[1, :, 128 * p : 128 * p + 128]
        even = jnp.where(left16, q, pltpu.roll(o, HEAD_DIM, 1))
        odd = jnp.where(left16, pltpu.roll(q, HEAD_DIM, 1), o)
        send_lat[2 * p, 0:16, :] = jnp.where(mine, even, 0.0).astype(BF16)
        send_lat[2 * p + 1, 0:16, :] = jnp.where(mine, odd, 0.0).astype(BF16)
    for h in range(HEADS):
        one, two, three = three_terms(dnorm_ref[h : h + 1, :])
        send_lat[h, 16:32, :] = jnp.where(
            rows16 == 0, one, jnp.where(rows16 == 1, two, jnp.where(rows16 == 2, three, 0.0))
        ).astype(BF16)

    for p in range(HEADS // 2):
        for i, ref in enumerate((keys_ref, grad_ref, values_ref)):
            turned = jnp.transpose(ref[:, 128 * p : 128 * p + 128])
            send_pts[2 * p, 64 * i : 64 * i + 64, :] = turned[0:64]
            send_pts[2 * p + 1, 64 * i : 64 * i + 64, :] = turned[64:128]

    pl.semaphore_wait(barrier, 2 * (SLOTS - 1))

    def lat_copy(h, src_slot):
        return remote(send_lat.at[h], got_lat.at[src_slot], s_lat.at[h], r_lat.at[src_slot], in_plane(h))

    def pts_copy(h, src_slot):
        return remote(send_pts.at[h], got_pts.at[src_slot], s_pts.at[h], r_pts.at[src_slot], in_plane(h))

    def to_heads(copy):
        def body(k):
            h = (slot + k) % SLOTS

            @pl.when(h < HEADS)
            def _():
                copy(h, slot).start()

        loop(1, SLOTS, body)

    to_heads(lat_copy)
    to_heads(pts_copy)

    @pl.when(slot < HEADS)
    def _():
        got_lat[slot] = send_lat[slot]
        got_pts[slot] = send_pts[slot]

        norm_row = enorm_ref[pl.ds(slot, 1), :]
        terms = three_terms(norm_row)

        def norm_block(g):
            cc, zz = g // 8, g % 8
            r = iota((BLOCK, 1024), 0)
            place = (r // 16) * 256 + (zz % 2) * 128 + cc * 64 + ((r // 4) % 4) * 16 + (zz // 2) * 4 + r % 4
            hot = jnp.where(iota((BLOCK, 1024), 1) == place, 1.0, 0.0).astype(BF16)
            total = jnp.zeros((BLOCK, 128), F32)
            for t in terms:
                wide = jnp.broadcast_to(t, (128, 1024)).astype(BF16)
                total = total + lax.dot_general(
                    hot, wide, (((1,), (1,)), ((), ())), preferred_element_type=F32
                )
            enorm[g] = total

        loop(0, SLOTS, norm_block)

        zero_rows = jnp.zeros((HEAD_DIM, NW), BF16)
        ones_rows = jnp.where(iota((HEAD_DIM, NW), 0) < 3, -1.0, 0.0).astype(BF16)
        for b in range(NB):
            key_rows[b, 64:128, :] = zero_rows
            grad_rows[b, 0:64, :] = zero_rows
            value_rows[b, 64:128, :] = ones_rows

        def lat_wait(k):
            lat_copy(slot, (slot + k) % SLOTS).wait_recv()

        loop(1, SLOTS, lat_wait)

        for i in range(4):
            total = got_lat[4 * i, 0:16, :].astype(F32)
            for j in range(1, 4):
                total = total + got_lat[4 * i + j, 0:16, :].astype(F32)
            lat[member, 16 * i : 16 * i + 16, :] = total.astype(BF16)

        def all_copy(buf, s, r, g_to, g_from):
            return remote(buf.at[g_from], buf.at[g_from], s.at[g_to], r.at[g_from], in_column(g_to))

        loop(1, SLOTS, lambda k: all_copy(lat, s_all, r_all, (member + k) % SLOTS, member).start())

        for t in range(SLOTS):
            dn = jnp.sum(got_lat[t, 16:32, :].astype(F32), axis=0, keepdims=True)
            dnorm[t // 4, :, 128 * (t % 4) : 128 * (t % 4) + 128] = jnp.broadcast_to(dn, (8, 128))

        def pts_wait(k):
            pts_copy(slot, (slot + k) % SLOTS).wait_recv()

        loop(1, SLOTS, pts_wait)

        for t in range(SLOTS):
            b, at = t // 4, 128 * (t % 4)
            key_rows[b, 0:64, at : at + 128] = got_pts[t, 0:64, :]
            grad_rows[b, 64:128, at : at + 128] = got_pts[t, 64:128, :]
            value_rows[b, 0:64, at : at + 128] = got_pts[t, 128:192, :]
            key_grad[b, at : at + 128, :] = jnp.transpose(got_pts[t, 0:128, :])
            value_cols[b, at : at + 128, 0:64] = jnp.transpose(got_pts[t, 128:192, :])
            value_cols[b, at : at + 128, 64:128] = jnp.zeros((128, 64), BF16)

        loop(1, SLOTS, lambda k: all_copy(lat, s_all, r_all, member, (member + k) % SLOTS).wait_recv())

        left = iota((CROWS, 128), 1) < HEAD_DIM

        def chunk_of(order):
            cc = (1 - c) if order < 2 else c
            far = order % 2 == 0
            zc = (1 - z // 4) if far else z // 4
            return cc, zc, cc * 2 + zc

        def core_copy(src, dst, s, r, cc, zc, order):
            g = cc * 8 + zc * 4
            return remote(
                src.at[pl.ds(g, CHUNK)], dst.at[pl.ds(zc * 4, CHUNK)], s.at[order], r.at[zc],
                in_column((1 - c) * 8 + z),
            )

        def z_copy(src, dst, s, r, z_to, z_from):
            return remote(src.at[z_to], dst.at[z_from], s.at[z_to], r.at[z_from], in_column(c * 8 + z_to))

        def scatter(order, part, core_got, total, z_got, s1, r1, s2, r2):
            cc, zc, _ = chunk_of(order)
            if order < 2:
                core_copy(part, core_got, s1, r1, cc, zc, order).start()
                return
            core_copy(part, core_got, s1, r1, cc, zc, order % 2).wait_recv()

            def send(i):
                zz = zc * 4 + i
                total[zz] = part[c * 8 + zz] + core_got[zz]

                @pl.when(zz != z)
                def _():
                    z_copy(total, z_got, s2, r2, zz, z).start()

                @pl.when(zz == z)
                def _():
                    z_got[z] = total[z]

            loop(0, CHUNK, send)

        def scatter_wait(z_got, total, s2, r2):
            loop(1, 8, lambda k: z_copy(total, z_got, s2, r2, z, (z + k) % 8).wait_recv())
            result = z_got[0]
            for i in range(1, 8):
                result = result + z_got[i]
            return result

        for order in range(4):
            cc, zc, ch = chunk_of(order)
            lat_c = lat[pl.ds(ch * CHUNK, CHUNK)].reshape(CROWS, 128)
            lat_turned[ch] = jnp.transpose(lat_c)[0:64]

            def block(b, accs):
                mix_acc, u_acc = accs
                scores = dot(lat[pl.ds(ch * CHUNK, CHUNK)].reshape(CROWS, 128), key_rows[b])
                d = jnp.exp(scores - dnorm[b, 0:1, :])
                e = jnp.exp(scores - enorm[pl.ds(ch * CHUNK, CHUNK)].reshape(CROWS, 128)[:, 0:1])
                dec[ch, b] = d
                enc[ch, b] = e
                mix_acc = mix_acc + dot(d.astype(BF16), key_grad[b])
                u_acc = u_acc + dot(e.astype(BF16), value_cols[b])
                return mix_acc, u_acc

            blank = jnp.zeros((CROWS, 128), F32)
            mix_acc, u_acc = lax.fori_loop(0, NB, block, (blank, blank))
            mixu[pl.ds(ch * CHUNK, CHUNK)] = jnp.where(left, u_acc, mix_acc).reshape(CHUNK, BLOCK, 128)
            scatter(order, mixu, from_core, summed, from_z, s_core, r_core, s_z, r_z)

        query_acc[...] = jnp.zeros((4, CROWS, 128), F32)

        def decoder_block(b):
            def totals(ch, total):
                dg = dot(lat[pl.ds(ch * CHUNK, CHUNK)].reshape(CROWS, 128), grad_rows[b])
                dgrad[ch] = dg
                return total + jnp.sum(dec[ch, b] * dg, axis=0, keepdims=True)

            row_total = lax.fori_loop(0, 4, totals, jnp.zeros((1, NW), F32))

            def grads(ch, acc):
                ds = (dec[ch, b] * (dgrad[ch] - row_total)).astype(BF16)
                query_acc[ch] = query_acc[ch] + dot(ds, key_grad[b])
                return acc + dot(lat_turned[ch], ds)

            keys_t[b] = lax.fori_loop(0, 4, grads, jnp.zeros((64, NW), F32))
            values_t[b] = jnp.zeros((64, NW), F32)

        loop(0, 1, decoder_block)

        own = scatter_wait(from_z, summed, s_z, r_z)
        lane = iota((BLOCK, 128), 1)
        mix_half = pltpu.roll(own, HEAD_DIM, 1).astype(BF16).astype(F32)
        column_total = jnp.sum(jnp.where(lane < HEAD_DIM, own * mix_half, 0.0), axis=1, keepdims=True)
        one, two, three = three_terms(column_total)
        mix_all[member] = jnp.where(
            lane < HEAD_DIM, mix_half,
            jnp.where(lane == 64, one, jnp.where(lane == 65, two, jnp.where(lane == 66, three, 0.0))),
        ).astype(BF16)
        loop(1, SLOTS, lambda k: all_copy(mix_all, s_mix, r_mix, (member + k) % SLOTS, member).start())

        loop(1, NB, decoder_block)

        loop(1, SLOTS, lambda k: all_copy(mix_all, s_mix, r_mix, member, (member + k) % SLOTS).wait_recv())

        for order in range(4):
            cc, zc, ch = chunk_of(order)
            mix_turned = jnp.transpose(mix_all[pl.ds(ch * CHUNK, CHUNK)].reshape(CROWS, 128))[0:64]

            def block2(b, acc):
                eg = dot(mix_all[pl.ds(ch * CHUNK, CHUNK)].reshape(CROWS, 128), value_rows[b])
                e = enc[ch, b]
                ds = (e * eg).astype(BF16)
                values_t[b] = values_t[b] + dot(mix_turned, e.astype(BF16))
                keys_t[b] = keys_t[b] + dot(lat_turned[ch], ds)
                return acc + dot(ds, key_grad[b])

            acc = lax.fori_loop(0, NB, block2, query_acc[ch]) * 0.125
            acc = acc.reshape(CHUNK, BLOCK, 128)
            upper = acc[:, 0:32, :].reshape(CHUNK * 32, 128)
            lower = pltpu.roll(acc[:, 32:64, :].reshape(CHUNK * 32, 128), HEAD_DIM, 1)
            packed = jnp.where(iota((CHUNK * 32, 128), 1) < HEAD_DIM, upper, lower)
            lg_part[pl.ds(ch * CHUNK, CHUNK)] = packed.reshape(CHUNK, 32, 128)
            scatter(order, lg_part, lg_core, lg_summed, lg_z, s_core2, r_core2, s_z2, r_z2)

        for t in range(SLOTS):
            b, at = t // 4, 128 * (t % 4)
            kv_send[t, 0:64, :] = keys_t[b, :, at : at + 128].astype(BF16)
            kv_send[t, 64:128, :] = values_t[b, :, at : at + 128].astype(BF16)

    def kv_copy(t, h):
        return remote(kv_send.at[t], kv_got.at[h], s_kv.at[t], r_kv.at[h], in_plane(t))

    def lg_copy(t, h):
        row = ((t // 4) % 2) * 16 + ((t % 4) // 2) * 8
        return remote(lg_own.at[pl.ds(row, 8)], lg_got.at[h], s_lg.at[t], r_lg.at[h], in_plane(t))

    @pl.when(slot < HEADS)
    def _():
        loop(1, SLOTS, lambda k: kv_copy((slot + k) % SLOTS, slot).start())
        kv_got[slot] = kv_send[slot]

        def z_copy2(z_to, z_from):
            return remote(
                lg_summed.at[z_to], lg_z.at[z_from], s_z2.at[z_to], r_z2.at[z_from], in_column(c * 8 + z_to)
            )

        loop(1, 8, lambda k: z_copy2(z, (z + k) % 8).wait_recv())
        result = lg_z[0]
        for i in range(1, 8):
            result = result + lg_z[i]
        lg_own[...] = result
        loop(1, SLOTS, lambda k: lg_copy((slot + k) % SLOTS, slot).start())
        row = pl.multiple_of((x % 2) * 16 + (y // 2) * 8, 8)
        lg_got[slot] = lg_own[pl.ds(row, 8), :]

    def from_heads(copy):
        def body(k):
            h = (slot + k) % SLOTS

            @pl.when(h < HEADS)
            def _():
                copy(slot, h).wait_recv()

        loop(1, SLOTS, body)

    from_heads(kv_copy)
    for p in range(HEADS // 2):
        for i, ref in enumerate((kout_ref, vout_ref)):
            both = jnp.concatenate(
                [kv_got[2 * p, 64 * i : 64 * i + 64, :], kv_got[2 * p + 1, 64 * i : 64 * i + 64, :]], axis=0
            )
            ref[:, 128 * p : 128 * p + 128] = jnp.transpose(both)

    from_heads(lg_copy)
    left8 = iota((8, 128), 1) < HEAD_DIM
    high = x // 2 == 1
    for p in range(HEADS // 2):
        a, b = lg_got[2 * p], lg_got[2 * p + 1]
        a = jnp.where(high, pltpu.roll(a, HEAD_DIM, 1), a)
        b = jnp.where(high, b, pltpu.roll(b, HEAD_DIM, 1))
        both = jnp.where(left8, a, b)
        lgout_ref[:, 128 * p : 128 * p + 128] = jnp.where(y % 2 == 0, both[0:4], both[4:8])

    def sent(k):
        h = (slot + k) % SLOTS

        @pl.when(h < HEADS)
        def _():
            lat_copy(h, slot).wait_send()
            pts_copy(h, slot).wait_send()

    loop(1, SLOTS, sent)

    @pl.when(slot < HEADS)
    def _():
        def sent_column(k):
            g = (member + k) % SLOTS
            remote(lat.at[member], lat.at[member], s_all.at[g], r_all.at[member], in_column(g)).wait_send()
            remote(mix_all.at[member], mix_all.at[member], s_mix.at[g], r_mix.at[member], in_column(g)).wait_send()
            t = (slot + k) % SLOTS
            kv_copy(t, slot).wait_send()
            lg_copy(t, slot).wait_send()

        loop(1, SLOTS, sent_column)

        def sent_z(k):
            zz = (z + k) % 8
            remote(summed.at[zz], from_z.at[z], s_z.at[zz], r_z.at[z], in_column(c * 8 + zz)).wait_send()
            remote(lg_summed.at[zz], lg_z.at[z], s_z2.at[zz], r_z2.at[z], in_column(c * 8 + zz)).wait_send()

        loop(1, 8, sent_z)
        sibling = in_column((1 - c) * 8 + z)
        for order in range(2):
            zc = (1 - z // 4) if order == 0 else z // 4
            g = (1 - c) * 8 + zc * 4
            remote(
                mixu.at[pl.ds(g, CHUNK)], from_core.at[pl.ds(zc * 4, CHUNK)], s_core.at[order], r_core.at[zc], sibling
            ).wait_send()
            remote(
                lg_part.at[pl.ds(g, CHUNK)], lg_core.at[pl.ds(zc * 4, CHUNK)], s_core2.at[order], r_core2.at[zc], sibling
            ).wait_send()


def shards(point_keys, point_values, out_grad, decoder_norm, latent_query, latent_out, encoder_norm):
    vmem = pl.BlockSpec(memory_space=pltpu.VMEM)
    sem = pltpu.SemaphoreType.DMA
    scratch = [
        pltpu.VMEM((HEADS, 32, 128), BF16),
        pltpu.VMEM((HEADS, 192, 128), BF16),
        pltpu.VMEM((2, 16, 768), F32),
        pltpu.VMEM((SLOTS, 32, 128), BF16),
        pltpu.VMEM((SLOTS, 192, 128), BF16),
        pltpu.VMEM((NB, 128, NW), BF16),
        pltpu.VMEM((NB, 128, NW), BF16),
        pltpu.VMEM((NB, 128, NW), BF16),
        pltpu.VMEM((NB, NW, 128), BF16),
        pltpu.VMEM((NB, NW, 128), BF16),
        pltpu.VMEM((NB, 8, NW), F32),
        pltpu.VMEM((SLOTS, BLOCK, 128), F32),
        pltpu.VMEM((SLOTS, BLOCK, 128), BF16),
        pltpu.VMEM((4, 64, CROWS), BF16),
        pltpu.VMEM((4, NB, CROWS, NW), F32),
        pltpu.VMEM((4, NB, CROWS, NW), F32),
        pltpu.VMEM((4, CROWS, NW), F32),
        pltpu.VMEM((4, CROWS, 128), F32),
        pltpu.VMEM((SLOTS, BLOCK, 128), F32),
        pltpu.VMEM((8, BLOCK, 128), F32),
        pltpu.VMEM((8, BLOCK, 128), F32),
        pltpu.VMEM((8, BLOCK, 128), F32),
        pltpu.VMEM((SLOTS, BLOCK, 128), BF16),
        pltpu.VMEM((NB, 64, NW), F32),
        pltpu.VMEM((NB, 64, NW), F32),
        pltpu.VMEM((SLOTS, 32, 128), F32),
        pltpu.VMEM((8, 32, 128), F32),
        pltpu.VMEM((8, 32, 128), F32),
        pltpu.VMEM((8, 32, 128), F32),
        pltpu.VMEM((32, 128), F32),
        pltpu.VMEM((SLOTS, 128, 128), BF16),
        pltpu.VMEM((HEADS, 128, 128), BF16),
        pltpu.VMEM((HEADS, 8, 128), F32),
        sem((SLOTS,)), sem((SLOTS,)), sem((SLOTS,)), sem((SLOTS,)),
        sem((SLOTS,)), sem((SLOTS,)), sem((2,)), sem((2,)), sem((8,)), sem((8,)),
        sem((SLOTS,)), sem((SLOTS,)), sem((2,)), sem((2,)), sem((8,)), sem((8,)),
        sem((SLOTS,)), sem((SLOTS,)), sem((SLOTS,)), sem((SLOTS,)),
    ]
    return pl.pallas_call(
        kernel,
        out_shape=(
            jax.ShapeDtypeStruct(point_keys.shape, BF16),
            jax.ShapeDtypeStruct(point_values.shape, BF16),
            jax.ShapeDtypeStruct(latent_query.shape, F32),
        ),
        in_specs=[vmem] * 7,
        out_specs=(vmem, vmem, vmem),
        scratch_shapes=scratch,
        compiler_params=pltpu.CompilerParams(
            collective_id=0, has_side_effects=True, vmem_limit_bytes=48 * 1024 * 1024
        ),
        name="routing_backward",
    )(point_keys, point_values, out_grad, decoder_norm, latent_query, latent_out, encoder_norm)


def solution(mesh):
    both = ("pa", "pb")
    rows = P(both, None)
    return jax.shard_map(
        shards,
        mesh=mesh,
        in_specs=(rows, rows, rows, P(None, both), rows, rows, P()),
        out_specs=(rows, rows, rows),
        check_vma=False,
    )
```

time: 1430 us -> 77.2 us (0.05)
  waiting for transfers between devices: 942 us -> 0 us
  blocking collectives: 229 us -> 0 us
  matrix products: 166 us -> 0 us
  Pallas kernels: 0 us -> 68.6 us
  local copies, waits for them, and re-layouts: 66.2 us -> 7.64 us
    all_gather x1 -> x0, waiting for transfers between devices: 682 us -> none  [in_one_piece(): result = lax.all_gather(both, axis, axis=dim, tiled=True)]
    unnamed x3 -> x0, waiting for transfers between devices: 261 us -> none
    psum x2 -> x0, blocking collectives: 229 us -> none  [the longest x1 155 us: shards(): mix_grad = lax.psum(mix_acc, ('pa', 'pb'))]
    dot_general x144 -> x0, matrix products: 166 us -> none  [the longest x72 79.1 us: across(): lax.dot_general(left, right, (((1,), (1,)), ((), ())), preferred_element_...]
    pallas_call x0 -> x1, Pallas kernels: none -> 68.6 us  [shards(): pl.pallas_call(kernel, out_shape=(jax.ShapeDtypeStruct(point_keys.shape,...]
    dynamic_slice x24 -> x0, local copies, waits for them, and re-layouts: 18.6 us -> none  [encoder_row(): return lax.dynamic_slice_in_dim(encoder_norm, current, 1, 0)]
    dynamic_update_slice x12 -> x0, local copies, waits for them, and re-layouts: 16.8 us -> none  [pass_two(): lax.dynamic_update_slice_in_dim(partial_rows, sums, current, 0)]
  transfers between devices with their start and end apart: 2 -> 0, of which waited for: 2 -> 0; matrix products, arithmetic and copies ran while one was open for 0% -> 0% of each run, Pallas kernels for 0% -> 0%
where the time goes in v1:
time: 77.2 us; the launch traced here: 76.9 us
  Pallas kernels  68.6 us (89%)
  local copies, waits for them, and re-layouts  7.64 us (10%)
    pallas_call x1, Pallas kernels, shards(): pl.pallas_call(kernel, out_shape=(jax.ShapeDtypeStruct(point_keys.shape,...  68.6 us
    unnamed x17, local copies, waits for them, and re-layouts  7.64 us

profile of v1, /device:TPU:8, one launch (start us, length us, event | category | flops | bytes accessed | tf_op | source)
XLA Modules:
  0.0 76.9 jit_solution(13643489139837352718)
XLA Ops:
  0.6 0.0 copy-start
  0.6 0.9 %copy-done = bf16[128,768]{1,0:T(8,128)(2,1)S(1)} copy-done((bf16[128,768]{1,0:T(8,128)(2,1)S(1)}, bf16[128,768]{1,0:T(8,128)(2,1)}, u32[]{:S(2)}) %copy-start) | copy-done | bytes 196632
  1.6 0.0 copy-start.1
  1.6 0.9 %copy-done.1 = bf16[128,768]{1,0:T(8,128)(2,1)S(1)} copy-done((bf16[128,768]{1,0:T(8,128)(2,1)S(1)}, bf16[128,768]{1,0:T(8,128)(2,1)}, u32[]{:S(2)}) %copy-start.1) | copy-done | bytes 196632
  2.5 0.0 copy-start.2
  2.5 0.9 %copy-done.2 = bf16[128,768]{1,0:T(8,128)(2,1)S(1)} copy-done((bf16[128,768]{1,0:T(8,128)(2,1)S(1)}, bf16[128,768]{1,0:T(8,128)(2,1)}, u32[]{:S(2)}) %copy-start.2) | copy-done | bytes 196632
  3.4 0.0 copy-start.3
  3.4 0.8 %copy-done.3 = f32[12,1024]{1,0:T(8,128)S(1)} copy-done((f32[12,1024]{1,0:T(8,128)S(1)}, f32[12,1024]{1,0:T(8,128)}, u32[]{:S(2)}) %copy-start.3) | copy-done | bytes 49176
  4.3 0.0 copy-start.4
  4.3 0.7 copy-done.4
  5.0 0.0 copy-start.5
  5.0 0.7 copy-done.5
  5.6 0.0 copy-start.6
  5.6 0.7 copy-done.6
  6.3 68.6 %routing_backward.1 = (bf16[128,768]{1,0:T(8,128)(2,1)S(1)}, bf16[128,768]{1,0:T(8,128)(2,1)S(1)}, f32[4,768]{1,0:T(4,128)S(1)}) custom-call(bf16[128,768]{1,0:T(8,128)(2,1)S(1)} %copy-done, bf16[128,768]{1,0:T(8,128)(2,1)S(1)} %copy-done.1, bf16[128,768]{1,0:T(8,128)(2,1)S(1)} %copy-done.2, f32[12,128]{1,0:T(8,128)S(1)} %copy-done.4, ...), custom_call_target="tpu_custom_call" | custom-call | tf_op jit(solution)/shard_map/routing_backward/pallas_call | solution.py:457
  75.0 0.7 copy.13
  75.6 0.7 copy.14
  76.3 0.6 copy.15
Async XLA Ops:
  0.6 0.9 %copy-start = (bf16[128,768]{1,0:T(8,128)(2,1)S(1)}, bf16[128,768]{1,0:T(8,128)(2,1)}, u32[]{:S(2)}) copy-start(bf16[128,768]{1,0:T(8,128)(2,1)} %keys_ref.1) | copy-start | bytes 589828
  1.6 0.9 %copy-start.1 = (bf16[128,768]{1,0:T(8,128)(2,1)S(1)}, bf16[128,768]{1,0:T(8,128)(2,1)}, u32[]{:S(2)}) copy-start(bf16[128,768]{1,0:T(8,128)(2,1)} %values_ref.1) | copy-start | bytes 589828
  2.5 0.9 %copy-start.2 = (bf16[128,768]{1,0:T(8,128)(2,1)S(1)}, bf16[128,768]{1,0:T(8,128)(2,1)}, u32[]{:S(2)}) copy-start(bf16[128,768]{1,0:T(8,128)(2,1)} %grad_ref.1) | copy-start | bytes 589828
  3.4 0.8 %copy-start.3 = (f32[12,1024]{1,0:T(8,128)S(1)}, f32[12,1024]{1,0:T(8,128)}, u32[]{:S(2)}) copy-start(f32[12,1024]{1,0:T(8,128)} %enorm_ref.1) | copy-start | bytes 147460
  4.3 0.7 copy-start.4
  5.0 0.7 copy-start.5
  5.6 0.7 copy-start.6

commit v2 on v1

v2 whole, which is shorter than its diff:
```python
import jax
import jax.numpy as jnp
from jax import lax
from jax.experimental import pallas as pl
from jax.experimental.pallas import tpu as pltpu
from jax.sharding import PartitionSpec as P

HEADS = 12
HEAD_DIM = 64
SLOTS = 16
PTS = 128
BLOCK = 64
CHUNK = 4
CROWS = CHUNK * BLOCK
NB = 4
NW = 512
Z_ORDER = (4, 3, 5, 2, 6, 1, 7)
PLANE_ORDER = (10, 9, 11, 6, 14, 5, 7, 13, 15, 2, 8, 1, 3, 4, 12)
MESH = pl.DeviceIdType.MESH
F32 = jnp.float32
BF16 = jnp.bfloat16


def dot(a, b):
    return jnp.dot(a, b, preferred_element_type=F32)


def dot_lanes(a, b):
    return lax.dot_general(a, b, (((1,), (1,)), ((), ())), preferred_element_type=F32)


def three_terms(v):
    one = v.astype(BF16).astype(F32)
    two = (v - one).astype(BF16).astype(F32)
    three = (v - one - two).astype(BF16).astype(F32)
    return one, two, three


def iota(shape, dim):
    return lax.broadcasted_iota(jnp.int32, shape, dim)


def head_at(place):
    x, lane = place // 4, (place // 4 + place % 4) % 4
    return jnp.where(lane < 3, 3 * x + lane, HEADS + x)


def kernel(
    keys_hbm, values_hbm, grad_hbm, dnorm_hbm, query_hbm, lout_hbm, enorm_hbm,
    kv_out, lg_out,
    keys_ref, values_ref, grad_ref, dnorm_ref, query_ref, lout_ref, enorm_ref, s_in,
    send_lat, send_pts, tall, got_lat, got_pts,
    dnorm, enorm,
    lat, lat_turned, dec, enc, dgrad, query_acc,
    mixu, from_core, summed, from_z, mix_all, keys_t, values_t,
    lg_part, lg_core, lg_summed, lg_z, lg_own, kv_send, kv_got, lg_got,
    s_lat, r_lat, s_pts, r_pts, s_all, r_all, s_core, r_core, s_z, r_z,
    s_mix, r_mix, s_core2, r_core2, s_z2, r_z2, s_kv, r_kv, s_lg, r_lg,
):
    inputs = [
        pltpu.make_async_copy(src, dst, s_in.at[i])
        for i, (src, dst) in enumerate((
            (query_hbm, query_ref), (lout_hbm, lout_ref), (dnorm_hbm, dnorm_ref), (keys_hbm, keys_ref),
            (grad_hbm, grad_ref), (values_hbm, values_ref), (enorm_hbm, enorm_ref),
        ))
    ]
    for copy in inputs:
        copy.start()
    pa, pb = lax.axis_index("pa"), lax.axis_index("pb")
    x, zlo, c = pa // 4, (pa // 2) % 2, pa % 2
    y, zhi = pb // 4, pb % 4
    z = zhi * 2 + zlo
    place = x * 4 + y
    head = head_at(place)
    member = c * 8 + z

    def in_plane(t):
        return ((t // 4) * 4 + zlo * 2 + c, (t % 4) * 4 + zhi)

    def in_column(g):
        cc, zz = g // 8, g % 8
        return (x * 4 + (zz % 2) * 2 + cc, y * 4 + zz // 2)

    def plane_at(k):
        return ((x + k // 4) % 4) * 4 + (y + k % 4) % 4

    def remote(src, dst, s, r, to):
        return pltpu.make_async_remote_copy(
            src_ref=src, dst_ref=dst, send_sem=s, recv_sem=r, device_id=to, device_id_type=MESH
        )

    def loop(lo, hi, body):
        def step(i, carry):
            body(i)
            return carry

        lax.fori_loop(lo, hi, step, 0)

    def along_z(buf, s, r, zz):
        return remote(buf.at[member], buf.at[member], s.at[zz], r.at[member], in_column(c * 8 + zz))

    def to_sibling(buf, s, r, zz):
        g = c * 8 + zz
        return remote(buf.at[g], buf.at[g], s.at[8 + zz], r.at[g], in_column((1 - c) * 8 + z))

    def arrival(buf, s, r, g):
        return remote(buf.at[g], buf.at[g], s.at[0], r.at[g], in_column((1 - c) * 8 + z))

    def gather_send(buf, s, r):
        for k in Z_ORDER:
            along_z(buf, s, r, (z + k) % 8).start()
        to_sibling(buf, s, r, z).start()

    def gather_relay(buf, s, r):
        for k in reversed(Z_ORDER):
            zz = (z + k) % 8
            arrival(buf, s, r, c * 8 + zz).wait_recv()
            to_sibling(buf, s, r, zz).start()

    def gather_sibling(buf, s, r, zc):
        for i in range(CHUNK):
            arrival(buf, s, r, (1 - c) * 8 + zc * 4 + i).wait_recv()

    barrier = pltpu.get_barrier_semaphore()

    def greet(k):
        pl.semaphore_signal(barrier, inc=1, device_id=in_plane((place + k) % SLOTS), device_id_type=MESH)
        pl.semaphore_signal(barrier, inc=1, device_id=in_column((member + k) % SLOTS), device_id_type=MESH)

    loop(1, SLOTS, greet)

    for copy in inputs[:3]:
        copy.wait()
    for k in range(4):
        tall[0, 4 * k : 4 * k + 4, :] = query_ref[...].astype(F32) * 0.125
        tall[1, 4 * k : 4 * k + 4, :] = lout_ref[...].astype(F32)
    rows16 = iota((16, 128), 0)
    left16 = iota((16, 128), 1) < HEAD_DIM
    mine = rows16 // 4 == y
    for p in range(HEADS // 2):
        q = tall[0, :, 128 * p : 128 * p + 128]
        o = tall[1, :, 128 * p : 128 * p + 128]
        even = jnp.where(left16, q, pltpu.roll(o, HEAD_DIM, 1))
        odd = jnp.where(left16, pltpu.roll(q, HEAD_DIM, 1), o)
        send_lat[2 * p] = jnp.where(mine, even, 0.0).astype(BF16)
        send_lat[2 * p + 1] = jnp.where(mine, odd, 0.0).astype(BF16)
    for h in range(HEADS):
        one, two, three = three_terms(dnorm_ref[h : h + 1, :])
        send_pts[h, 0:16, :] = jnp.where(
            rows16 == 0, one, jnp.where(rows16 == 1, two, jnp.where(rows16 == 2, three, 0.0))
        ).astype(BF16)

    for copy in inputs[3:]:
        copy.wait()
    for p in range(HEADS // 2):
        for i, ref in enumerate((keys_ref, grad_ref, values_ref)):
            turned = jnp.transpose(ref[:, 128 * p : 128 * p + 128])
            send_pts[2 * p, 64 * i + 16 : 64 * i + 80, :] = turned[0:64]
            send_pts[2 * p + 1, 64 * i + 16 : 64 * i + 80, :] = turned[64:128]

    pl.semaphore_wait(barrier, 2 * (SLOTS - 1))

    def lat_copy(to, src):
        h = head_at(to)
        return remote(send_lat.at[h], got_lat.at[src], s_lat.at[h], r_lat.at[src], in_plane(to))

    def pts_copy(to, src):
        h = head_at(to)
        return remote(send_pts.at[h], got_pts.at[src, pl.ds(0, 208)], s_pts.at[h], r_pts.at[src], in_plane(to))

    def to_heads(copy, order=PLANE_ORDER):
        for k in order:
            to = plane_at(k)

            @pl.when(head_at(to) < HEADS)
            def _():
                copy(to, place).start()

    to_heads(lat_copy)
    to_heads(pts_copy, PLANE_ORDER[:1])

    @pl.when(head >= HEADS)
    def _():
        to_heads(pts_copy, PLANE_ORDER[1:])

    @pl.when(head < HEADS)
    def _():
        got_lat[place] = send_lat[head]
        got_pts[place, 0:208, :] = send_pts[head]

        norm_row = enorm_ref[pl.ds(head, 1), :]
        terms = three_terms(norm_row)

        def norm_block(g):
            cc, zz = g // 8, g % 8
            r = iota((BLOCK, 1024), 0)
            place = (r // 16) * 256 + (zz % 2) * 128 + cc * 64 + ((r // 4) % 4) * 16 + (zz // 2) * 4 + r % 4
            hot = jnp.where(iota((BLOCK, 1024), 1) == place, 1.0, 0.0).astype(BF16)
            total = jnp.zeros((BLOCK, 128), F32)
            for t in terms:
                wide = jnp.broadcast_to(t, (128, 1024)).astype(BF16)
                total = total + lax.dot_general(
                    hot, wide, (((1,), (1,)), ((), ())), preferred_element_type=F32
                )
            enorm[g] = total


        ones_rows = jnp.where(iota((HEAD_DIM, 128), 0) < 3, -1.0, 0.0).astype(BF16)
        for t in range(SLOTS):
            got_pts[t, 208:272, :] = ones_rows

        def lat_wait(k):
            src = (place + k) % SLOTS
            remote(send_lat.at[0], got_lat.at[src], s_lat.at[0], r_lat.at[src], in_plane(src)).wait_recv()

        loop(1, SLOTS, lat_wait)

        for i in range(4):
            total = got_lat[4 * i].astype(F32)
            for j in range(1, 4):
                total = total + got_lat[4 * i + j].astype(F32)
            lat[member, 16 * i : 16 * i + 16, :] = total.astype(BF16)

        gather_send(lat, s_all, r_all)
        to_heads(pts_copy, PLANE_ORDER[1:])
        loop(0, SLOTS, norm_block)

        gather_relay(lat, s_all, r_all)

        def pts_wait(k):
            src = (place + k) % SLOTS
            remote(
                send_pts.at[0], got_pts.at[src, pl.ds(0, 208)], s_pts.at[0], r_pts.at[src], in_plane(src)
            ).wait_recv()

        loop(1, SLOTS, pts_wait)

        for t in range(SLOTS):
            dn = jnp.sum(got_pts[t, 0:16, :].astype(F32), axis=0, keepdims=True)
            dnorm[t // 4, :, 128 * (t % 4) : 128 * (t % 4) + 128] = jnp.broadcast_to(dn, (8, 128))

        left = iota((CROWS, 128), 1) < HEAD_DIM

        lane_c = iota((CROWS, 128), 1)

        def wide(lo, hi, b):
            return jnp.concatenate([got_pts[4 * b + i, lo:hi, :] for i in range(4)], axis=1)

        def queries(ch):
            both = lat[pl.ds(ch * CHUNK, CHUNK)].reshape(CROWS, 128)
            return jnp.where(lane_c < HEAD_DIM, both, jnp.zeros_like(both))

        def outs(ch):
            both = lat[pl.ds(ch * CHUNK, CHUNK)].reshape(CROWS, 128)
            return jnp.where(lane_c < HEAD_DIM, jnp.zeros_like(both), both)

        def chunk_of(order):
            cc = c if order in (0, 3) else 1 - c
            zc = 1 - z // 4 if order < 2 else z // 4
            return cc, zc, cc * 2 + zc

        def core_copy(src, dst, s, r, cc, zc, order):
            g = cc * 8 + zc * 4
            return remote(
                src.at[pl.ds(g, CHUNK)], dst.at[pl.ds(zc * 4, CHUNK)], s.at[order], r.at[zc],
                in_column((1 - c) * 8 + z),
            )

        def z_copy(src, dst, s, r, z_to, z_from):
            return remote(src.at[z_to], dst.at[z_from], s.at[z_to], r.at[z_from], in_column(c * 8 + z_to))

        def scatter(order, part, core_got, total, z_got, s1, r1, s2, r2):
            if order == 0:
                return
            if order < 3:
                cc, zc, _ = chunk_of(order)
                core_copy(part, core_got, s1, r1, cc, zc, order - 1).start()
                if order == 1:
                    return
            cc, zc, _ = chunk_of(0 if order == 2 else 3)
            core_copy(part, core_got, s1, r1, cc, zc, 0).wait_recv()

            def send(i):
                zz = zc * 4 + i
                total[zz] = part[c * 8 + zz] + core_got[zz]

                @pl.when(zz != z)
                def _():
                    z_copy(total, z_got, s2, r2, zz, z).start()

                @pl.when(zz == z)
                def _():
                    z_got[z] = total[z]

            loop(0, CHUNK, send)

        def scatter_wait(z_got, total, s2, r2):
            loop(1, 8, lambda k: z_copy(total, z_got, s2, r2, z, (z + k) % 8).wait_recv())
            result = z_got[0]
            for i in range(1, 8):
                result = result + z_got[i]
            return result

        for order in range(4):
            cc, zc, ch = chunk_of(order)
            if order in (1, 2):
                gather_sibling(lat, s_all, r_all, zc)
            lat_c = lat[pl.ds(ch * CHUNK, CHUNK)].reshape(CROWS, 128)
            lat_turned[ch] = jnp.transpose(lat_c)[0:64]

            def block(b, accs):
                mix_acc, u_acc = accs
                keys_grads = wide(16, 144, b)
                scores = dot(queries(ch), keys_grads)
                d = jnp.exp(scores - dnorm[b, 0:1, :])
                e = jnp.exp(scores - enorm[pl.ds(ch * CHUNK, CHUNK)].reshape(CROWS, 128)[:, 0:1])
                dec[ch, b] = d
                enc[ch, b] = e
                mix_acc = mix_acc + dot_lanes(d.astype(BF16), keys_grads)
                u_acc = u_acc + dot_lanes(e.astype(BF16), wide(144, 272, b))
                return mix_acc, u_acc

            blank = jnp.zeros((CROWS, 128), F32)
            mix_acc, u_acc = lax.fori_loop(0, NB, block, (blank, blank))
            mixu[pl.ds(ch * CHUNK, CHUNK)] = jnp.where(left, u_acc, mix_acc).reshape(CHUNK, BLOCK, 128)
            scatter(order, mixu, from_core, summed, from_z, s_core, r_core, s_z, r_z)

        query_acc[...] = jnp.zeros((4, CROWS, 128), F32)

        def decoder_block(b):
            def totals(ch, total):
                dg = dot(outs(ch), wide(16, 144, b))
                dgrad[ch] = dg
                return total + jnp.sum(dec[ch, b] * dg, axis=0, keepdims=True)

            row_total = lax.fori_loop(0, 4, totals, jnp.zeros((1, NW), F32))

            def grads(ch, acc):
                ds = (dec[ch, b] * (dgrad[ch] - row_total)).astype(BF16)
                query_acc[ch] = query_acc[ch] + dot_lanes(ds, wide(16, 144, b))
                return acc + dot(lat_turned[ch], ds)

            keys_t[b] = lax.fori_loop(0, 4, grads, jnp.zeros((64, NW), F32))
            values_t[b] = jnp.zeros((64, NW), F32)

        loop(0, 1, decoder_block)

        own = scatter_wait(from_z, summed, s_z, r_z)
        lane = iota((BLOCK, 128), 1)
        mix_half = pltpu.roll(own, HEAD_DIM, 1).astype(BF16).astype(F32)
        column_total = jnp.sum(jnp.where(lane < HEAD_DIM, own * mix_half, 0.0), axis=1, keepdims=True)
        one, two, three = three_terms(column_total)
        mix_all[member] = jnp.where(
            lane < HEAD_DIM, mix_half,
            jnp.where(lane == 64, one, jnp.where(lane == 65, two, jnp.where(lane == 66, three, 0.0))),
        ).astype(BF16)
        gather_send(mix_all, s_mix, r_mix)

        loop(1, NB, decoder_block)

        gather_relay(mix_all, s_mix, r_mix)

        for order in range(4):
            cc, zc, ch = chunk_of(order)
            if order in (1, 2):
                gather_sibling(mix_all, s_mix, r_mix, zc)
            mix_turned = jnp.transpose(mix_all[pl.ds(ch * CHUNK, CHUNK)].reshape(CROWS, 128))[0:64]

            def block2(b, acc):
                eg = dot(mix_all[pl.ds(ch * CHUNK, CHUNK)].reshape(CROWS, 128), wide(144, 272, b))
                e = enc[ch, b]
                ds = (e * eg).astype(BF16)
                values_t[b] = values_t[b] + dot(mix_turned, e.astype(BF16))
                keys_t[b] = keys_t[b] + dot(lat_turned[ch], ds)
                return acc + dot_lanes(ds, wide(16, 144, b))

            acc = lax.fori_loop(0, NB, block2, query_acc[ch]) * 0.125
            acc = acc.reshape(CHUNK, BLOCK, 128)
            upper = acc[:, 0:32, :].reshape(CHUNK * 32, 128)
            lower = pltpu.roll(acc[:, 32:64, :].reshape(CHUNK * 32, 128), HEAD_DIM, 1)
            packed = jnp.where(iota((CHUNK * 32, 128), 1) < HEAD_DIM, upper, lower)
            lg_part[pl.ds(ch * CHUNK, CHUNK)] = packed.reshape(CHUNK, 32, 128)
            scatter(order, lg_part, lg_core, lg_summed, lg_z, s_core2, r_core2, s_z2, r_z2)

        for t in range(SLOTS):
            b, at = t // 4, 128 * (t % 4)
            kv_send[t, 0:64, :] = keys_t[b, :, at : at + 128].astype(BF16)
            kv_send[t, 64:128, :] = values_t[b, :, at : at + 128].astype(BF16)

    def kv_copy(t, h):
        return remote(kv_send.at[t], kv_got.at[h], s_kv.at[t], r_kv.at[h], in_plane(t))

    def lg_copy(t, h):
        row = ((t // 4) % 2) * 16 + ((t % 4) // 2) * 8
        return remote(lg_own.at[pl.ds(row, 8)], lg_got.at[h], s_lg.at[t], r_lg.at[h], in_plane(t))

    @pl.when(head < HEADS)
    def _():
        loop(1, SLOTS, lambda k: kv_copy((place + k) % SLOTS, head).start())
        kv_got[head] = kv_send[place]

        def z_copy2(z_to, z_from):
            return remote(
                lg_summed.at[z_to], lg_z.at[z_from], s_z2.at[z_to], r_z2.at[z_from], in_column(c * 8 + z_to)
            )

        loop(1, 8, lambda k: z_copy2(z, (z + k) % 8).wait_recv())
        result = lg_z[0]
        for i in range(1, 8):
            result = result + lg_z[i]
        lg_own[...] = result
        for k in PLANE_ORDER:
            lg_copy(plane_at(k), head).start()
        row = pl.multiple_of((x % 2) * 16 + (y // 2) * 8, 8)
        lg_got[head] = lg_own[pl.ds(row, 8), :]

    def from_heads(copy):
        def body(k):
            src = (place + k) % SLOTS

            @pl.when(head_at(src) < HEADS)
            def _():
                copy(place, head_at(src)).wait_recv()

        loop(1, SLOTS, body)

    from_heads(kv_copy)
    kv_out[...] = kv_got[...]
    from_heads(lg_copy)
    lg_out[...] = lg_got[...]

    def sent(k):
        to = (place + k) % SLOTS

        @pl.when(head_at(to) < HEADS)
        def _():
            lat_copy(to, place).wait_send()
            pts_copy(to, place).wait_send()

    loop(1, SLOTS, sent)

    @pl.when(head < HEADS)
    def _():
        def sent_column(k):
            t = (place + k) % SLOTS
            kv_copy(t, head).wait_send()
            lg_copy(t, head).wait_send()

        loop(1, SLOTS, sent_column)
        to_sibling(lat, s_all, r_all, z).wait_send()
        to_sibling(mix_all, s_mix, r_mix, z).wait_send()

        def sent_z(k):
            zz = (z + k) % 8
            for buf, s, r in ((lat, s_all, r_all), (mix_all, s_mix, r_mix)):
                along_z(buf, s, r, zz).wait_send()
                to_sibling(buf, s, r, zz).wait_send()
            remote(summed.at[zz], from_z.at[z], s_z.at[zz], r_z.at[z], in_column(c * 8 + zz)).wait_send()
            remote(lg_summed.at[zz], lg_z.at[z], s_z2.at[zz], r_z2.at[z], in_column(c * 8 + zz)).wait_send()

        loop(1, 8, sent_z)
        sibling = in_column((1 - c) * 8 + z)
        for order in range(2):
            zc = (1 - z // 4) if order == 0 else z // 4
            g = (1 - c) * 8 + zc * 4
            remote(
                mixu.at[pl.ds(g, CHUNK)], from_core.at[pl.ds(zc * 4, CHUNK)], s_core.at[order], r_core.at[zc], sibling
            ).wait_send()
            remote(
                lg_part.at[pl.ds(g, CHUNK)], lg_core.at[pl.ds(zc * 4, CHUNK)], s_core2.at[order], r_core2.at[zc], sibling
            ).wait_send()


def unpack(kv_ref, lg_ref, kout_ref, vout_ref, lgout_ref):
    pa, pb = lax.axis_index("pa"), lax.axis_index("pb")
    high, y = pa // 8 == 1, pb // 4
    for p in range(HEADS // 2):
        for i, ref in enumerate((kout_ref, vout_ref)):
            both = jnp.concatenate(
                [kv_ref[2 * p, 64 * i : 64 * i + 64, :], kv_ref[2 * p + 1, 64 * i : 64 * i + 64, :]], axis=0
            )
            ref[:, 128 * p : 128 * p + 128] = jnp.transpose(both)
    left8 = iota((8, 128), 1) < HEAD_DIM
    for p in range(HEADS // 2):
        a, b = lg_ref[2 * p], lg_ref[2 * p + 1]
        a = jnp.where(high, pltpu.roll(a, HEAD_DIM, 1), a)
        b = jnp.where(high, b, pltpu.roll(b, HEAD_DIM, 1))
        both = jnp.where(left8, a, b)
        lgout_ref[:, 128 * p : 128 * p + 128] = jnp.where(y % 2 == 0, both[0:4], both[4:8])


def shards(point_keys, point_values, out_grad, decoder_norm, latent_query, latent_out, encoder_norm):
    vmem = pl.BlockSpec(memory_space=pltpu.VMEM)
    sem = pltpu.SemaphoreType.DMA
    scratch = [
        pltpu.VMEM((PTS, 768), BF16), pltpu.VMEM((PTS, 768), BF16), pltpu.VMEM((PTS, 768), BF16),
        pltpu.VMEM((HEADS, PTS), F32), pltpu.VMEM((4, 768), BF16), pltpu.VMEM((4, 768), BF16),
        pltpu.VMEM((HEADS, 1024), F32), sem((7,)),
        pltpu.VMEM((HEADS, 16, 128), BF16),
        pltpu.VMEM((HEADS, 208, 128), BF16),
        pltpu.VMEM((2, 16, 768), F32),
        pltpu.VMEM((SLOTS, 16, 128), BF16),
        pltpu.VMEM((SLOTS, 272, 128), BF16),
        pltpu.VMEM((NB, 8, NW), F32),
        pltpu.VMEM((SLOTS, BLOCK, 128), F32),
        pltpu.VMEM((SLOTS, BLOCK, 128), BF16),
        pltpu.VMEM((4, 64, CROWS), BF16),
        pltpu.VMEM((4, NB, CROWS, NW), F32),
        pltpu.VMEM((4, NB, CROWS, NW), F32),
        pltpu.VMEM((4, CROWS, NW), F32),
        pltpu.VMEM((4, CROWS, 128), F32),
        pltpu.VMEM((SLOTS, BLOCK, 128), F32),
        pltpu.VMEM((8, BLOCK, 128), F32),
        pltpu.VMEM((8, BLOCK, 128), F32),
        pltpu.VMEM((8, BLOCK, 128), F32),
        pltpu.VMEM((SLOTS, BLOCK, 128), BF16),
        pltpu.VMEM((NB, 64, NW), F32),
        pltpu.VMEM((NB, 64, NW), F32),
        pltpu.VMEM((SLOTS, 32, 128), F32),
        pltpu.VMEM((8, 32, 128), F32),
        pltpu.VMEM((8, 32, 128), F32),
        pltpu.VMEM((8, 32, 128), F32),
        pltpu.VMEM((32, 128), F32),
        pltpu.VMEM((SLOTS, 128, 128), BF16),
        pltpu.VMEM((HEADS, 128, 128), BF16),
        pltpu.VMEM((HEADS, 8, 128), F32),
        sem((SLOTS,)), sem((SLOTS,)), sem((SLOTS,)), sem((SLOTS,)),
        sem((SLOTS,)), sem((SLOTS,)), sem((2,)), sem((2,)), sem((8,)), sem((8,)),
        sem((SLOTS,)), sem((SLOTS,)), sem((2,)), sem((2,)), sem((8,)), sem((8,)),
        sem((SLOTS,)), sem((SLOTS,)), sem((SLOTS,)), sem((SLOTS,)),
    ]
    kv, lg = pl.pallas_call(
        kernel,
        out_shape=(
            pltpu.VMEM((HEADS, 128, 128), BF16),
            pltpu.VMEM((HEADS, 8, 128), F32),
        ),
        in_specs=[pl.BlockSpec(memory_space=pl.ANY)] * 7,
        out_specs=(vmem, vmem),
        scratch_shapes=scratch,
        compiler_params=pltpu.CompilerParams(
            collective_id=0, has_side_effects=True, vmem_limit_bytes=56 * 1024 * 1024
        ),
        name="routing_backward",
    )(point_keys, point_values, out_grad, decoder_norm, latent_query, latent_out, encoder_norm)
    return pl.pallas_call(
        unpack,
        out_shape=(
            jax.ShapeDtypeStruct(point_keys.shape, BF16),
            jax.ShapeDtypeStruct(point_values.shape, BF16),
            jax.ShapeDtypeStruct(latent_query.shape, F32),
        ),
        in_specs=[vmem] * 2,
        out_specs=(vmem, vmem, vmem),
        compiler_params=pltpu.CompilerParams(vmem_limit_bytes=8 * 1024 * 1024),
        name="unpack",
    )(kv, lg)


def solution(mesh):
    both = ("pa", "pb")
    rows = P(both, None)
    return jax.shard_map(
        shards,
        mesh=mesh,
        in_specs=(rows, rows, rows, P(None, both), rows, rows, P()),
        out_specs=(rows, rows, rows),
        check_vma=False,
    )
```

time: 77.2 us -> 66.1 us (0.86)
  local copies, waits for them, and re-layouts: 7.64 us -> 0 us
  Pallas kernels: 68.6 us -> 65.3 us
    unnamed x17 -> x0, local copies, waits for them, and re-layouts: 7.64 us -> none
    pallas_call x1 -> x2, Pallas kernels: 68.6 us -> 65.3 us  [the longest x1 64.4 us: shards(): pl.pallas_call(kernel, out_shape=(pltpu.VMEM((HEADS, 128, 128), BF16), pl...]
where the time goes in v2:
time: 66.1 us; the launch traced here: 66 us
  Pallas kernels  65.3 us (99%)
    pallas_call x1, Pallas kernels, shards(): pl.pallas_call(kernel, out_shape=(pltpu.VMEM((HEADS, 128, 128), BF16), pl...  64.4 us

profile of v2, /device:TPU:8, one launch (start us, length us, event | category | flops | bytes accessed | tf_op | source)
XLA Modules:
  0.0 66.0 jit_solution(16870256340849991895)
XLA Ops:
  0.6 64.4 %routing_backward.1 = (bf16[12,128,128]{2,1,0:T(8,128)(2,1)S(1)}, f32[12,8,128]{2,1,0:T(8,128)S(1)}) custom-call(bf16[128,768]{1,0:T(8,128)(2,1)} %keys_hbm.1, bf16[128,768]{1,0:T(8,128)(2,1)} %values_hbm.1, bf16[128,768]{1,0:T(8,128)(2,1)} %grad_hbm.1, f32[12,128]{1,0:T(8,128)} %dnorm_hbm.1, bf16[4,768]{1,0:T(4,128)(2,1)} %query_hbm.1, ...), custom_call_target="tpu_custom_call" | custom-call | tf_op jit(solution)/shard_map/routing_backward/pallas_call | solution.py:532
  65.0 0.9 %unpack.1 = (bf16[128,768]{1,0:T(8,128)(2,1)}, bf16[128,768]{1,0:T(8,128)(2,1)}, f32[4,768]{1,0:T(4,128)}) custom-call(bf16[12,128,128]{2,1,0:T(8,128)(2,1)S(1)} %get-tuple-element.5.kv_ref, f32[12,8,128]{2,1,0:T(8,128)S(1)} %get-tuple-element.6.lg_ref), custom_call_target="tpu_custom_call" | custom-call | tf_op jit(solution)/shard_map/unpack/pallas_call | solution.py:546

commit v3 on v2

--- a/solution.py
+++ b/solution.py
@@ -12,8 +12,8 @@
 BLOCK = 64
 CHUNK = 4
 CROWS = CHUNK * BLOCK
-NB = 4
-NW = 512
+NB = 1
+NW = 2048
 Z_ORDER = (4, 3, 5, 2, 6, 1, 7)
 PLANE_ORDER = (10, 9, 11, 6, 14, 5, 7, 13, 15, 2, 8, 1, 3, 4, 12)
 MESH = pl.DeviceIdType.MESH
@@ -52,9 +52,9 @@
     send_lat, send_pts, tall, got_lat, got_pts,
     dnorm, enorm,
     lat, lat_turned, dec, enc, dgrad, query_acc,
-    mixu, from_core, summed, from_z, mix_all, keys_t, values_t,
+    mixu, from_core, summed, from_z, summed_u, from_z_u, mix_all, keys_t, values_t,
     lg_part, lg_core, lg_summed, lg_z, lg_own, kv_send, kv_got, lg_got,
-    s_lat, r_lat, s_pts, r_pts, s_all, r_all, s_core, r_core, s_z, r_z,
+    s_lat, r_lat, s_pts, r_pts, s_all, r_all, s_core, r_core, s_z, r_z, s_zu, r_zu,
     s_mix, r_mix, s_core2, r_core2, s_z2, r_z2, s_kv, r_kv, s_lg, r_lg,
 ):
     inputs = [
@@ -237,14 +237,14 @@
 
         for t in range(SLOTS):
             dn = jnp.sum(got_pts[t, 0:16, :].astype(F32), axis=0, keepdims=True)
-            dnorm[t // 4, :, 128 * (t % 4) : 128 * (t % 4) + 128] = jnp.broadcast_to(dn, (8, 128))
+            dnorm[t // 16, :, 128 * (t % 16) : 128 * (t % 16) + 128] = jnp.broadcast_to(dn, (8, 128))
 
         left = iota((CROWS, 128), 1) < HEAD_DIM
 
         lane_c = iota((CROWS, 128), 1)
 
         def wide(lo, hi, b):
-            return jnp.concatenate([got_pts[4 * b + i, lo:hi, :] for i in range(4)], axis=1)
+            return jnp.concatenate([got_pts[16 * b + i, lo:hi, :] for i in range(16)], axis=1)
 
         def queries(ch):
             both = lat[pl.ds(ch * CHUNK, CHUNK)].reshape(CROWS, 128)
@@ -269,7 +269,25 @@
         def z_copy(src, dst, s, r, z_to, z_from):
             return remote(src.at[z_to], dst.at[z_from], s.at[z_to], r.at[z_from], in_column(c * 8 + z_to))
 
-        def scatter(order, part, core_got, total, z_got, s1, r1, s2, r2):
+        left32 = iota((32, 128), 1) < HEAD_DIM
+
+        def mixu_send(zz):
+            both = mixu[c * 8 + zz] + from_core[zz]
+            upper, lower = both[0:32], pltpu.roll(both[32:64], HEAD_DIM, 1)
+            summed[zz] = jnp.where(left32, lower, upper)
+            summed_u[zz] = jnp.where(left32, upper, lower).astype(BF16)
+
+            @pl.when(zz != z)
+            def _():
+                z_copy(summed, from_z, s_z, r_z, zz, z).start()
+                z_copy(summed_u, from_z_u, s_zu, r_zu, zz, z).start()
+
+            @pl.when(zz == z)
+            def _():
+                from_z[z] = summed[z]
+                from_z_u[z] = summed_u[z]
+
+        def scatter(order, part, core_got, total, z_got, s1, r1, s2, r2, send_one=None):
             if order == 0:
                 return
             if order < 3:
@@ -282,7 +300,7 @@
 
             def send(i):
                 zz = zc * 4 + i
-                total[zz] = part[c * 8 + zz] + core_got[zz]
+                total[zz] = (part[c * 8 + zz] + core_got[zz]).astype(total.dtype)
 
                 @pl.when(zz != z)
                 def _():
@@ -292,13 +310,13 @@
                 def _():
                     z_got[z] = total[z]
 
-            loop(0, CHUNK, send)
+            loop(0, CHUNK, send if send_one is None else lambda i: send_one(zc * 4 + i))
 
         def scatter_wait(z_got, total, s2, r2):
             loop(1, 8, lambda k: z_copy(total, z_got, s2, r2, z, (z + k) % 8).wait_recv())
-            result = z_got[0]
+            result = z_got[0].astype(F32)
             for i in range(1, 8):
-                result = result + z_got[i]
+                result = result + z_got[i].astype(F32)
             return result
 
         for order in range(4):
@@ -323,7 +341,7 @@
             blank = jnp.zeros((CROWS, 128), F32)
             mix_acc, u_acc = lax.fori_loop(0, NB, block, (blank, blank))
             mixu[pl.ds(ch * CHUNK, CHUNK)] = jnp.where(left, u_acc, mix_acc).reshape(CHUNK, BLOCK, 128)
-            scatter(order, mixu, from_core, summed, from_z, s_core, r_core, s_z, r_z)
+            scatter(order, mixu, from_core, summed, from_z, s_core, r_core, s_z, r_z, mixu_send)
 
         query_acc[...] = jnp.zeros((4, CROWS, 128), F32)
 
@@ -343,11 +361,12 @@
             keys_t[b] = lax.fori_loop(0, 4, grads, jnp.zeros((64, NW), F32))
             values_t[b] = jnp.zeros((64, NW), F32)
 
-        loop(0, 1, decoder_block)
-
-        own = scatter_wait(from_z, summed, s_z, r_z)
+
+        own_mix = scatter_wait(from_z, summed, s_z, r_z)
+        own_u = scatter_wait(from_z_u, summed_u, s_zu, r_zu)
         lane = iota((BLOCK, 128), 1)
-        mix_half = pltpu.roll(own, HEAD_DIM, 1).astype(BF16).astype(F32)
+        mix_half = jnp.concatenate([pltpu.roll(own_mix, HEAD_DIM, 1), own_mix], axis=0).astype(BF16).astype(F32)
+        own = jnp.concatenate([own_u, pltpu.roll(own_u, HEAD_DIM, 1)], axis=0)
         column_total = jnp.sum(jnp.where(lane < HEAD_DIM, own * mix_half, 0.0), axis=1, keepdims=True)
         one, two, three = three_terms(column_total)
         mix_all[member] = jnp.where(
@@ -356,7 +375,7 @@
         ).astype(BF16)
         gather_send(mix_all, s_mix, r_mix)
 
-        loop(1, NB, decoder_block)
+        loop(0, NB, decoder_block)
 
         gather_relay(mix_all, s_mix, r_mix)
 
@@ -383,7 +402,7 @@
             scatter(order, lg_part, lg_core, lg_summed, lg_z, s_core2, r_core2, s_z2, r_z2)
 
         for t in range(SLOTS):
-            b, at = t // 4, 128 * (t % 4)
+            b, at = t // 16, 128 * (t % 16)
             kv_send[t, 0:64, :] = keys_t[b, :, at : at + 128].astype(BF16)
             kv_send[t, 64:128, :] = values_t[b, :, at : at + 128].astype(BF16)
 
@@ -456,6 +475,7 @@
                 along_z(buf, s, r, zz).wait_send()
                 to_sibling(buf, s, r, zz).wait_send()
             remote(summed.at[zz], from_z.at[z], s_z.at[zz], r_z.at[z], in_column(c * 8 + zz)).wait_send()
+            remote(summed_u.at[zz], from_z_u.at[z], s_zu.at[zz], r_zu.at[z], in_column(c * 8 + zz)).wait_send()
             remote(lg_summed.at[zz], lg_z.at[z], s_z2.at[zz], r_z2.at[z], in_column(c * 8 + zz)).wait_send()
 
         loop(1, 8, sent_z)
@@ -511,8 +531,10 @@
         pltpu.VMEM((4, CROWS, 128), F32),
         pltpu.VMEM((SLOTS, BLOCK, 128), F32),
         pltpu.VMEM((8, BLOCK, 128), F32),
-        pltpu.VMEM((8, BLOCK, 128), F32),
-        pltpu.VMEM((8, BLOCK, 128), F32),
+        pltpu.VMEM((8, 32, 128), F32),
+        pltpu.VMEM((8, 32, 128), F32),
+        pltpu.VMEM((8, 32, 128), BF16),
+        pltpu.VMEM((8, 32, 128), BF16),
         pltpu.VMEM((SLOTS, BLOCK, 128), BF16),
         pltpu.VMEM((NB, 64, NW), F32),
         pltpu.VMEM((NB, 64, NW), F32),
@@ -525,7 +547,7 @@
         pltpu.VMEM((HEADS, 128, 128), BF16),
         pltpu.VMEM((HEADS, 8, 128), F32),
         sem((SLOTS,)), sem((SLOTS,)), sem((SLOTS,)), sem((SLOTS,)),
-        sem((SLOTS,)), sem((SLOTS,)), sem((2,)), sem((2,)), sem((8,)), sem((8,)),
+        sem((SLOTS,)), sem((SLOTS,)), sem((2,)), sem((2,)), sem((8,)), sem((8,)), sem((8,)), sem((8,)),
         sem((SLOTS,)), sem((SLOTS,)), sem((2,)), sem((2,)), sem((8,)), sem((8,)),
         sem((SLOTS,)), sem((SLOTS,)), sem((SLOTS,)), sem((SLOTS,)),
     ]

time: 66.1 us -> 60.4 us (0.914); the launches traced: 66 us -> 59.4 us
  Pallas kernels: 65.3 us -> 58.7 us
    pallas_call x1, Pallas kernels: 64.4 us -> 57.8 us  [shards(): pl.pallas_call(kernel, out_shape=(pltpu.VMEM((HEADS, 128, 128), BF16), pl...]
where the time goes in v3:
time: 60.4 us; the launch traced here: 59.4 us
  Pallas kernels  58.7 us (97%)
  between operations  0.64 us (1%)
    pallas_call x1, Pallas kernels, shards(): pl.pallas_call(kernel, out_shape=(pltpu.VMEM((HEADS, 128, 128), BF16), pl...  57.8 us

profile of v3, /device:TPU:8, one launch (start us, length us, event | category | flops | bytes accessed | tf_op | source)
XLA Modules:
  0.0 59.4 jit_solution(16451803797698458697)
XLA Ops:
  0.6 57.8 %routing_backward.1 = (bf16[12,128,128]{2,1,0:T(8,128)(2,1)S(1)}, f32[12,8,128]{2,1,0:T(8,128)S(1)}) custom-call(bf16[128,768]{1,0:T(8,128)(2,1)} %keys_hbm.1, bf16[128,768]{1,0:T(8,128)(2,1)} %values_hbm.1, bf16[128,768]{1,0:T(8,128)(2,1)} %grad_hbm.1, f32[12,128]{1,0:T(8,128)} %dnorm_hbm.1, bf16[4,768]{1,0:T(4,128)(2,1)} %query_hbm.1, ...), custom_call_target="tpu_custom_call" | custom-call | tf_op jit(solution)/shard_map/routing_backward/pallas_call | solution.py:554
  58.4 0.9 %unpack.1 = (bf16[128,768]{1,0:T(8,128)(2,1)}, bf16[128,768]{1,0:T(8,128)(2,1)}, f32[4,768]{1,0:T(4,128)}) custom-call(bf16[12,128,128]{2,1,0:T(8,128)(2,1)S(1)} %get-tuple-element.5.kv_ref, f32[12,8,128]{2,1,0:T(8,128)S(1)} %get-tuple-element.6.lg_ref), custom_call_target="tpu_custom_call" | custom-call | tf_op jit(solution)/shard_map/unpack/pallas_call | solution.py:568
